TPU v7x, 512 devices: a whole 4x4x16 slice. The times are simulated.
512 devices in a mesh: feat: 16 (over x, y), label: 32 (over z, core).
Axes of the slice: x: 4, y: 4, z: 16, core: 2. Of those that a mesh axis runs over, the one named last changes fastest.
Arguments:
- doc_blocks: int32 [384, 8], replicated, may hold values from 0 to 511, all different within a row
- doc_counts: int32 [384], replicated, may hold values from 1 to 8
- doc_values: bfloat16 [384, 8, 256], replicated, may hold values from 0.049804688 to 2
- pos_labels: int32 [384, 8], replicated, may hold values from 0 to 131071, as said below
- neg_labels: int32 [384, 24], replicated, may hold values from 0 to 131071, as said below
- in_weight: bfloat16 [512, 256, 2048], P('feat', None, 'label'), may hold values from -0.1875 to 0.1875
- out_weight: bfloat16 [131072, 2048], P(('feat', 'label')), may hold values from -0.29882812 to 0.29882812
Outputs:
- in_grad: bfloat16 [512, 256, 2048], P('feat', None, 'label')
- out_grad: bfloat16 [131072, 2048], P(('feat', 'label'))
Inputs may be any that keep to these rules, and one draw needn't show every extreme that they name: The ids in one row of doc_blocks are distinct. `pos_labels`: label c is held by the device of linear index c // 256 (feat index times the size of label plus label index); taken together with neg_labels, every device's labels are named by exactly 24 of the listed pairs. `neg_labels`: see pos_labels.
All inputs are finite; a program needn't handle non-finite values.
Results may differ from a plain program's by a relative error of at most 0.0065.
Values may be sent and summed in bfloat16 or wider, within the bound.
No kernel may reach another device: no remote copies, remote signals or barrier semaphores. Data moves between devices by JAX's collectives and lax.ppermute only.
A program may use at most 128 MiB of HBM per device.

v0:
```python
import jax
import jax.numpy as jnp
from jax import lax
from jax.sharding import PartitionSpec as P


def on_device(doc_blocks, doc_counts, doc_values, pos_labels, neg_labels, in_weight, out_weight):
    block_count, block_size, col_count = in_weight.shape
    doc_total, slot_count = doc_blocks.shape
    lab_count = out_weight.shape[0]
    feat_index = lax.axis_index("feat")
    label_index = lax.axis_index("label")
    label_size = lax.axis_size("label")
    first_block = feat_index * block_count
    local_ids = doc_blocks - first_block
    slots = jnp.arange(slot_count, dtype=jnp.int32)
    valid = slots[None, :] < doc_counts[:, None]
    picks = (
        local_ids[:, :, None] == jnp.arange(block_count, dtype=jnp.int32)[None, None, :]
    ) & valid[:, :, None]
    dense = jnp.einsum(
        "dkb,dkv->dbv", picks.astype(jnp.bfloat16), doc_values, preferred_element_type=jnp.float32
    )
    flat_inputs = dense.astype(jnp.bfloat16).reshape(doc_total, block_count * block_size)
    weight_flat = in_weight.reshape(block_count * block_size, col_count)
    partial_value = jnp.dot(flat_inputs, weight_flat, preferred_element_type=jnp.float32)
    pre = lax.psum(partial_value, "feat")
    hidden_part = jax.nn.silu(pre).astype(jnp.bfloat16)
    hidden = lax.all_gather(hidden_part, "label", axis=1, tiled=True)
    logit = lax.dot_general(
        hidden, out_weight, (((1,), (1,)), ((), ())), preferred_element_type=jnp.float32
    )
    device_index = feat_index * label_size + label_index
    first_label = device_index * lab_count
    local_labels = jnp.arange(lab_count, dtype=jnp.int32)[None, None, :] + first_label
    pos_count = jnp.sum((pos_labels[:, :, None] == local_labels).astype(jnp.float32), axis=1)
    neg_count = jnp.sum((neg_labels[:, :, None] == local_labels).astype(jnp.float32), axis=1)
    sig = jax.nn.sigmoid(logit)
    grad_pos = (sig - 1.0).astype(jnp.bfloat16).astype(jnp.float32)
    grad_neg = sig.astype(jnp.bfloat16).astype(jnp.float32)
    label_grad = (pos_count * grad_pos + neg_count * grad_neg).astype(jnp.bfloat16)
    out_grad = lax.dot_general(
        label_grad, hidden, (((0,), (0,)), ((), ())), preferred_element_type=jnp.float32
    ).astype(jnp.bfloat16)
    grad_terms = jnp.dot(label_grad, out_weight, preferred_element_type=jnp.float32)
    summed = lax.psum(grad_terms, ("feat", "label"))
    hidden_grad = lax.dynamic_slice_in_dim(summed, label_index * col_count, col_count, 1)
    gate = jax.nn.sigmoid(pre)
    pre_grad = (hidden_grad * gate * (1.0 + pre * (1.0 - gate))).astype(jnp.bfloat16)
    in_flat = lax.dot_general(
        flat_inputs, pre_grad, (((0,), (0,)), ((), ())), preferred_element_type=jnp.float32
    )
    in_grad = in_flat.astype(jnp.bfloat16).reshape(block_count, block_size, col_count)
    return (in_grad, out_grad)


def solution(mesh):
    placed = (P(), P(), P(), P(), P(), P("feat", None, "label"), P(("feat", "label"), None))
    return jax.shard_map(
        on_device,
        mesh=mesh,
        in_specs=placed,
        out_specs=(P("feat", None, "label"), P(("feat", "label"), None)),
        check_vma=False,
    )
```

profile of v0, /device:TPU:2, one launch (start us, length us, event | category | flops | bytes accessed | tf_op | source)
XLA Modules:
  0.0 713.3 jit_solution(14605121180167996716)
XLA Ops:
  7.2 0.0 all-reduce.3.cloned.1.call-start
  7.2 0.8 broadcast_subtract_fusion
  8.1 0.1 copy.14
  8.2 0.8 iota_compare_fusion.1
  9.0 3.8 convolution_convert_fusion.1
  12.9 2.6 copy-done.1
  15.5 7.4 %fusion.7 = f32[384,64]{0,1:T(8,128)} fusion(bf16[32,256,64]{1,2,0:T(8,128)(2,1)S(1)} %copy-done.7, bf16[384,32,256]{2,1,0:T(8,128)(2,1)S(1)} %convolution_convert_fusion.1), kind=kOutput, calls=%fused_computation.13 | convolution fusion | flops 402653184 | bytes 7438336 | tf_op jit(solution)/shard_map/dot_general | solution.py:26
  22.9 0.0 all-reduce.3.cloned.1.call-update
  22.9 0.0 all-gather.2.cloned.1.call-start
  23.0 116.3 %all-reduce.3.cloned.1.call-done = f32[384,64]{0,1:T(8,128)} async-done(((f32[384,64]{0,1:T(8,128)}), f32[384,64]{0,1:T(8,128)}) %all-reduce.3.cloned.1.call-update) | async-done | bytes 98320 | tf_op jit(solution)/shard_map/psum | solution.py:27
  139.3 1.6 multiply_convert_fusion.1
  140.9 0.0 all-reduce.5.cloned.1.call-start
  140.9 0.1 copy.17
  141.1 0.1 copy.15
  141.2 2.9 convert_reduce_fusion.1
  144.1 3.1 convert_reduce_fusion
  147.2 66.0 %all-gather.2.cloned.1.call-done = bf16[384,2048]{0,1:T(8,128)(2,1)} async-done(((bf16[384,64]{0,1:T(8,128)(2,1)}), bf16[384,2048]{0,1:T(8,128)(2,1)}) %all-gather.2.cloned.1.call-update) | async-done | bytes 1572880 | tf_op jit(solution)/shard_map/all_gather | solution.py:29
  213.2 2.2 add_convert_fusion
  215.4 2.4 fusion.15
  217.9 12.9 %copy.20 = bf16[48,8,32,256]{3,1,2,0:T(8,128)(2,1)} copy(bf16[48,8,32,256]{3,2,1,0:T(8,128)(2,1)} %bitcast.18) | data formatting | bytes 12582912
  230.8 1.7 convolution_convert_fusion.2
  232.5 469.0 %all-reduce.5.cloned.1.call-done = f32[384,2048]{0,1:T(8,128)} async-done(((f32[384,2048]{0,1:T(8,128)}), f32[384,2048]{0,1:T(8,128)}) %all-reduce.5.cloned.1.call-update) | async-done | bytes 3145744 | tf_op jit(solution)/shard_map/psum | solution.py:46
  701.5 4.1 convolution_convert_fusion
  705.6 1.1 copy.26
  (18 shorter events, 0.1 us)
Async XLA Ops:
  7.2 1.8 copy-start
  7.2 132.1 %all-reduce.3.cloned.1.call-start = ((), (), s32[]{:S(2)}) async-start(), calls=%async_computation | async-start | bytes 196608 | tf_op jit(solution)/shard_map/psum | solution.py:27
  9.0 6.5 copy-start.7
  12.8 2.6 copy-start.1
  15.5 125.4 %copy-start.5 = (s32[384,24]{0,1:T(8,128)S(1)}, s32[384,24]{0,1:T(8,128)}, u32[]{:S(2)}) copy-start(s32[384,24]{0,1:T(8,128)} %param.11) | copy-start | bytes 110596
  15.5 125.6 %copy-start.6 = (s32[384,8]{0,1:T(8,128)S(1)}, s32[384,8]{0,1:T(8,128)}, u32[]{:S(2)}) copy-start(s32[384,8]{0,1:T(8,128)} %param.10) | copy-start | bytes 36868
  15.5 197.7 %copy-start.3 = (bf16[256,2048]{1,0:T(8,128)(2,1)S(1)}, bf16[256,2048]{1,0:T(8,128)(2,1)}, u32[]{:S(2)}) copy-start(bf16[256,2048]{1,0:T(8,128)(2,1)} %param.13) | copy-start | bytes 3145732
  22.9 190.2 %all-gather.2.cloned.1.call-start = ((), (), s32[]{:S(2)}) async-start(), calls=%async_computation.1 | async-start | bytes 1622016 | tf_op jit(solution)/shard_map/all_gather | solution.py:29
  140.9 560.7 %all-reduce.5.cloned.1.call-start = ((), (), s32[]{:S(2)}) async-start(), calls=%async_computation.2 | async-start | bytes 6291456 | tf_op jit(solution)/shard_map/psum | solution.py:46
  217.8 12.9 %copy-start.2 = (bf16[384,2048]{0,1:T(8,128)(2,1)S(1)}, bf16[384,2048]{0,1:T(8,128)(2,1)}, u32[]{:S(2)}) copy-start(bf16[384,2048]{0,1:T(8,128)(2,1)} %all-gather.2.cloned.1.call-done) | copy-start | bytes 4718596
  217.9 483.7 %copy-start.4 = (f32[384,64]{0,1:T(8,128)S(1)}, f32[384,64]{0,1:T(8,128)}, u32[]{:S(2)}) copy-start(f32[384,64]{0,1:T(8,128)} %all-reduce.3.cloned.1.call-done) | copy-start | bytes 294916
Sparse Core Ops, SparseCore 0:
  23.1 116.1 all-reduce.2
  141.6 71.4 all-gather.1
  219.3 482.1 all-reduce.4
where the time goes:
time: 713 us
  waiting for transfers between devices  651 us (91%)
  matrix products  21.7 us (3%)
  local copies, waits for them, and re-layouts  17 us (2%)
  between operations  13.9 us (2%)
  other arithmetic  9.17 us (1%)
    psum x1, waiting for transfers between devices, on_device(): summed = lax.psum(grad_terms, ('feat', 'label'))  469 us
    psum x1, waiting for transfers between devices, on_device(): pre = lax.psum(partial_value, 'feat')  116 us
    all_gather x1, waiting for transfers between devices, on_device(): hidden = lax.all_gather(hidden_part, 'label', axis=1, tiled=True)  66 us
    unnamed x19, local copies, waits for them, and re-layouts  15.8 us
  transfers between devices with their start and end apart: 3, of which 3 were waited for; matrix products, arithmetic and copies ran while one was open for 3% of the time, Pallas kernels for 0%

commit v1 on v0

--- a/solution.py
+++ b/solution.py
@@ -43,7 +43,7 @@
         label_grad, hidden, (((0,), (0,)), ((), ())), preferred_element_type=jnp.float32
     ).astype(jnp.bfloat16)
     grad_terms = jnp.dot(label_grad, out_weight, preferred_element_type=jnp.float32)
-    summed = lax.psum(grad_terms, ("feat", "label"))
+    summed = lax.psum(lax.psum(grad_terms, "label"), "feat")
     hidden_grad = lax.dynamic_slice_in_dim(summed, label_index * col_count, col_count, 1)
     gate = jax.nn.sigmoid(pre)
     pre_grad = (hidden_grad * gate * (1.0 + pre * (1.0 - gate))).astype(jnp.bfloat16)

time: 713 us -> 574 us (0.81)
  the two profiles are of different devices: /device:TPU:2 before, /device:TPU:1 now
where the time goes in v1:
time: 574 us
  waiting for transfers between devices  512 us (89%)
  matrix products  21.7 us (4%)
  local copies, waits for them, and re-layouts  17 us (3%)
  between operations  13.9 us (2%)
  other arithmetic  9.17 us (2%)
    psum x2, waiting for transfers between devices, on_device(): summed = lax.psum(lax.psum(grad_terms, 'label'), 'feat')  328 us
    psum x1, waiting for transfers between devices, on_device(): pre = lax.psum(partial_value, 'feat')  116 us
    all_gather x1, waiting for transfers between devices, on_device(): hidden = lax.all_gather(hidden_part, 'label', axis=1, tiled=True)  67 us
    unnamed x19, local copies, waits for them, and re-layouts  15.8 us
  transfers between devices with their start and end apart: 4, of which 4 were waited for; matrix products, arithmetic and copies ran while one was open for 4% of the time, Pallas kernels for 0%

profile of v1, /device:TPU:1, one launch (start us, length us, event | category | flops | bytes accessed | tf_op | source)
XLA Modules:
  0.0 574.1 jit_solution(7643906058983431294)
XLA Ops:
  7.2 0.8 broadcast_subtract_fusion
  8.1 0.1 copy.14
  8.2 0.8 iota_compare_fusion.1
  9.0 3.8 convolution_convert_fusion.1
  12.9 2.6 copy-done.1
  15.5 7.4 %fusion.7 = f32[384,64]{0,1:T(8,128)} fusion(bf16[32,256,64]{1,2,0:T(8,128)(2,1)S(1)} %copy-done.7, bf16[384,32,256]{2,1,0:T(8,128)(2,1)S(1)} %convolution_convert_fusion.1), kind=kOutput, calls=%fused_computation.13 | convolution fusion | flops 402653184 | bytes 7438336 | tf_op jit(solution)/shard_map/dot_general | solution.py:26
  22.9 0.0 all-gather.2.cloned.1.call-start
  23.0 116.5 %all-reduce.4.cloned.1.call-done = f32[384,64]{0,1:T(8,128)} async-done(((f32[384,64]{0,1:T(8,128)}), f32[384,64]{0,1:T(8,128)}) %all-reduce.4.cloned.1.call-update) | async-done | bytes 98320 | tf_op jit(solution)/shard_map/psum | solution.py:27
  139.5 1.6 multiply_convert_fusion.1
  141.1 0.0 all-reduce.6.cloned.1.call-start
  141.1 0.1 copy.17
  141.3 0.1 copy.15
  141.4 2.9 convert_reduce_fusion.1
  144.3 3.1 convert_reduce_fusion
  147.4 67.0 %all-gather.2.cloned.1.call-done = bf16[384,2048]{0,1:T(8,128)(2,1)} async-done(((bf16[384,64]{0,1:T(8,128)(2,1)}), bf16[384,2048]{0,1:T(8,128)(2,1)}) %all-gather.2.cloned.1.call-update) | async-done | bytes 1572880 | tf_op jit(solution)/shard_map/all_gather | solution.py:29
  214.4 2.2 add_convert_fusion
  216.7 2.4 fusion.15
  219.1 0.2 all-reduce.8.cloned.1.call-start
  219.4 213.9 %all-reduce.6.cloned.1.call-done = f32[384,2048]{0,1:T(8,128)} async-done(((f32[384,2048]{0,1:T(8,128)}), f32[384,2048]{0,1:T(8,128)}) %all-reduce.6.cloned.1.call-update) | async-done | bytes 3145744 | tf_op jit(solution)/shard_map/psum | solution.py:46
  433.3 12.9 %copy.20 = bf16[48,8,32,256]{3,1,2,0:T(8,128)(2,1)} copy(bf16[48,8,32,256]{3,2,1,0:T(8,128)(2,1)} %bitcast.18) | data formatting | bytes 12582912
  446.2 1.7 convolution_convert_fusion.2
  448.0 114.4 %all-reduce.8.cloned.1.call-done = f32[384,2048]{0,1:T(8,128)} async-done(((f32[384,2048]{0,1:T(8,128)}), f32[384,2048]{0,1:T(8,128)}) %all-reduce.8.cloned.1.call-update) | async-done | bytes 3145744 | tf_op jit(solution)/shard_map/psum | solution.py:46
  562.4 4.1 convolution_convert_fusion
  566.5 1.1 copy.26
  (21 shorter events, 0.1 us)
Async XLA Ops:
  7.2 1.8 copy-start
  7.2 132.3 %all-reduce.4.cloned.1.call-start = ((), (), s32[]{:S(2)}) async-start(), calls=%async_computation | async-start | bytes 196608 | tf_op jit(solution)/shard_map/psum | solution.py:27
  9.0 6.5 %copy-start.7 = (bf16[32,256,64]{1,2,0:T(8,128)(2,1)S(1)}, bf16[32,256,64]{1,2,0:T(8,128)(2,1)}, u32[]{:S(2)}) copy-start(bf16[32,256,64]{1,2,0:T(8,128)(2,1)} %param.12) | copy-start | bytes 3145732
  12.8 2.6 copy-start.1
  15.5 125.6 %copy-start.5 = (s32[384,24]{0,1:T(8,128)S(1)}, s32[384,24]{0,1:T(8,128)}, u32[]{:S(2)}) copy-start(s32[384,24]{0,1:T(8,128)} %param.11) | copy-start | bytes 110596
  15.5 125.8 %copy-start.6 = (s32[384,8]{0,1:T(8,128)S(1)}, s32[384,8]{0,1:T(8,128)}, u32[]{:S(2)}) copy-start(s32[384,8]{0,1:T(8,128)} %param.10) | copy-start | bytes 36868
  15.5 198.9 %copy-start.3 = (bf16[256,2048]{1,0:T(8,128)(2,1)S(1)}, bf16[256,2048]{1,0:T(8,128)(2,1)}, u32[]{:S(2)}) copy-start(bf16[256,2048]{1,0:T(8,128)(2,1)} %param.13) | copy-start | bytes 3145732
  22.9 191.5 %all-gather.2.cloned.1.call-start = ((), (), s32[]{:S(2)}) async-start(), calls=%async_computation.1 | async-start | bytes 1622016 | tf_op jit(solution)/shard_map/all_gather | solution.py:29
  141.1 292.2 %all-reduce.6.cloned.1.call-start = ((), (), s32[]{:S(2)}) async-start(), calls=%async_computation.2 | async-start | bytes 6291456 | tf_op jit(solution)/shard_map/psum | solution.py:46
  219.1 343.2 %all-reduce.8.cloned.1.call-start = ((), (), s32[]{:S(2)}) async-start(), calls=%async_computation.3 | async-start | bytes 6291456 | tf_op jit(solution)/shard_map/psum | solution.py:46
  433.3 12.9 %copy-start.2 = (bf16[384,2048]{0,1:T(8,128)(2,1)S(1)}, bf16[384,2048]{0,1:T(8,128)(2,1)}, u32[]{:S(2)}) copy-start(bf16[384,2048]{0,1:T(8,128)(2,1)} %all-gather.2.cloned.1.call-done) | copy-start | bytes 4718596
  433.3 129.0 %copy-start.4 = (f32[384,64]{0,1:T(8,128)S(1)}, f32[384,64]{0,1:T(8,128)}, u32[]{:S(2)}) copy-start(f32[384,64]{0,1:T(8,128)} %all-reduce.4.cloned.1.call-done) | copy-start | bytes 294916
Sparse Core Ops, SparseCore 0:
  23.1 116.3 all-reduce.3
  141.8 72.5 all-gather.1
  219.3 213.9 all-reduce.5
  436.5 125.8 all-reduce.7
